TPU v7x, 32 devices: a whole 2x2x4 slice. The times are simulated.
32 devices in a mesh: row: 8 (over z, y), col: 4 (over x, core).
Axes of the slice: x: 2, y: 2, z: 4, core: 2. Of those that a mesh axis runs over, the one named last changes fastest.
Arguments:
- feature_map: bfloat16 [512, 32, 2048], P('row', 'col'), may hold values from -6 to 6
- image_ids: int32 [512, 32], P('row', 'col'), may hold values from 0 to 16
- point_weight: bfloat16 [2048, 256], replicated, may hold values from -0.125 to 0.125
- atrous_weight: bfloat16 [3, 3, 3, 2048, 256], replicated, may hold values from -0.046875 to 0.046875
- pool_weight: bfloat16 [2048, 256], replicated, may hold values from -0.125 to 0.125
- project_weight: bfloat16 [1280, 256], replicated, may hold values from -0.15625 to 0.15625
- bn_gain: float32 [6, 256], replicated, may hold values from 0.5 to 1.5
- bn_shift: float32 [6, 256], replicated, may hold values from -2.5 to 2.5
- out_grad: bfloat16 [512, 32, 256], P('row', 'col'), may hold values from -6 to 6
Outputs:
- output: bfloat16 [512, 32, 256], P('row', 'col')
- input_grad: bfloat16 [512, 32, 2048], P('row', 'col')
- point_grad: float32 [2048, 256], P('row')
- atrous_grad: float32 [3, 3, 3, 2048, 256], P(None, None, None, 'row')
- pool_grad: float32 [2048, 256], P('row')
- project_grad: float32 [1280, 256], replicated
- gain_grad: float32 [6, 256], replicated
- shift_grad: float32 [6, 256], replicated
All inputs are finite; a program needn't handle non-finite values.
Results may differ from a plain program's by a relative error of at most 0.012.
Values may be sent and summed in bfloat16 or wider, within the bound.
No kernel may reach another device: no remote copies, remote signals or barrier semaphores. Data moves between devices by JAX's collectives and lax.ppermute only.
A program may use at most 448 MiB of HBM per device.

v0:
```python
import jax
import jax.numpy as jnp
from jax import lax
from jax.sharding import PartitionSpec as P

REACH = 18
IMG_ROWS = 32


EPSILON = 1e-05


def padded(x, sides, width):
    for axis, dim in sides:
        count, length = (lax.axis_size(axis), x.shape[dim])
        up = [(i, (i + 1) % count) for i in range(count - 1)]
        down = [(j, i) for i, j in up]
        last = lax.slice_in_dim(x, length - width, length, axis=dim)
        leading = lax.slice_in_dim(x, 0, width, axis=dim)
        before = lax.ppermute(last, axis, up)
        after = lax.ppermute(leading, axis, down)
        x = jnp.concatenate([before, x, after], axis=dim)
    return x


def smooth(value):
    return jax.nn.gelu(value, approximate=True)


def smooth_back(value, grad):
    _, backward = jax.vjp(smooth, value)
    return backward(grad)[0]


def moments(value):
    return jnp.stack([jnp.sum(value, axis=0), jnp.sum(value * value, axis=0)])


def per_device(
    feature_map,
    image_ids,
    point_weight,
    atrous_weight,
    pool_weight,
    project_weight,
    bn_gain,
    bn_shift,
    out_grad,
):
    rows, cols, chans = feature_map.shape
    feat = point_weight.shape[1]
    pixels = rows * cols
    reach = REACH
    row_count = lax.axis_size("row")
    total = float(pixels * row_count * lax.axis_size("col"))
    images = rows * row_count // IMG_ROWS + 1
    start_col = lax.axis_index("col") * cols
    marks = image_ids + 1
    own_marks = marks.reshape(pixels, 1)
    flat = feature_map.reshape(pixels, chans)
    local_ids = image_ids.reshape(pixels)
    wide, wide_marks = (
        lax.all_gather(feature_map, "col", axis=1, tiled=True),
        lax.all_gather(marks, "col", axis=1, tiled=True),
    )
    tall, tall_marks = (
        padded(wide, (("row", 0),), reach),
        padded(wide_marks, (("row", 0),), reach),
    )
    window = jnp.pad(tall, ((0, 0), (reach, reach), (0, 0)))
    window_marks = jnp.pad(tall_marks, ((0, 0), (reach, reach)))

    def offsets(branch, tap):
        spread = reach * (branch + 1) // 3
        return ((tap // 3 - 1) * spread, (tap % 3 - 1) * spread)

    def shifted(down, right):
        piece = lax.dynamic_slice(
            window, (reach + down, reach + right + start_col, 0), (rows, cols, chans)
        )
        return piece.reshape(pixels, chans)

    keeps = []
    branch_out = [jnp.dot(flat, point_weight, preferred_element_type=jnp.float32)]
    for branch in range(3):
        summed = jnp.zeros((pixels, feat), jnp.float32)
        for tap in range(9):
            down, right = offsets(branch, tap)
            near = lax.dynamic_slice(
                window_marks, (reach + down, reach + right + start_col), (rows, cols)
            )
            keep = (near.reshape(pixels, 1) == own_marks).astype(jnp.float32)
            keeps.append(keep)
            product = jnp.dot(
                shifted(down, right),
                atrous_weight[branch, tap // 3, tap % 3],
                preferred_element_type=jnp.float32,
            )
            summed = summed + keep * product
        branch_out.append(summed)
    table = local_ids[:, None] == jnp.arange(images, dtype=jnp.int32)[None, :]
    table_float = table.astype(jnp.float32)
    part_sums = jnp.einsum(
        "pi,pc->ic", table.astype(jnp.bfloat16), flat, preferred_element_type=jnp.float32
    )
    part_counts = jnp.sum(table_float, axis=0)
    image_sums, counts, first_stats = lax.psum(
        (part_sums, part_counts, jnp.stack([moments(v) for v in branch_out])), ("row", "col")
    )
    pooled = (image_sums / counts[:, None]).astype(jnp.bfloat16)
    per_image = jnp.dot(pooled, pool_weight, preferred_element_type=jnp.float32)
    branch_out.append(jnp.take(per_image, local_ids, axis=0))
    weighted = counts[:, None] * per_image
    pool_stats = jnp.stack([jnp.sum(weighted, axis=0), jnp.sum(weighted * per_image, axis=0)])
    stats = jnp.concatenate([first_stats, pool_stats[None]], axis=0)
    means = stats[:, 0] / total
    scales = lax.rsqrt(stats[:, 1] / total - means * means + EPSILON)
    normed = [(value - means[k]) * scales[k] for k, value in enumerate(branch_out)]
    lifted = [value * bn_gain[k] + bn_shift[k] for k, value in enumerate(normed)]
    joined = jnp.concatenate([smooth(value) for value in lifted], axis=1).astype(jnp.bfloat16)
    head = jnp.dot(joined, project_weight, preferred_element_type=jnp.float32)
    head_stats = lax.psum(moments(head), ("row", "col"))
    head_mean = head_stats[0] / total
    head_scale = lax.rsqrt(head_stats[1] / total - head_mean * head_mean + EPSILON)
    head_norm = (head - head_mean) * head_scale
    head_lift = head_norm * bn_gain[5] + bn_shift[5]
    output = smooth(head_lift).astype(jnp.bfloat16).reshape(rows, cols, feat)
    head_grad = smooth_back(head_lift, out_grad.reshape(pixels, feat).astype(jnp.float32))
    head_back = lax.psum(
        jnp.stack([jnp.sum(head_grad, axis=0), jnp.sum(head_grad * head_norm, axis=0)]),
        ("row", "col"),
    )
    head_slope = (
        bn_gain[5]
        * head_scale
        * (head_grad - head_back[0] / total - head_norm * head_back[1] / total)
    ).astype(jnp.bfloat16)
    project_part = jnp.einsum("pk,pf->kf", joined, head_slope, preferred_element_type=jnp.float32)
    joined_grad = jnp.dot(head_slope, project_weight.T, preferred_element_type=jnp.float32)
    grads = [smooth_back(lifted[k], joined_grad[:, k * feat : (k + 1) * feat]) for k in range(5)]
    back_moments = jnp.stack(
        [
            jnp.stack([jnp.sum(g, axis=0), jnp.sum(g * normed[k], axis=0)])
            for k, g in enumerate(grads)
        ]
    )
    rear, project_grad = lax.psum((back_moments, project_part), ("row", "col"))
    pool_pixel = (
        bn_gain[4] * scales[4] * (grads[4] - rear[4, 0] / total - normed[4] * rear[4, 1] / total)
    )
    local_image = jnp.einsum("pi,pf->if", table_float, pool_pixel, precision=lax.Precision.HIGHEST)
    image_slope = lax.psum(local_image, ("row", "col"))
    image_low = image_slope.astype(jnp.bfloat16)
    pool_full = jnp.einsum("ic,if->cf", pooled, image_low, preferred_element_type=jnp.float32)
    row_share = chans // row_count
    pool_grad = lax.dynamic_slice_in_dim(pool_full, lax.axis_index("row") * row_share, row_share, 0)
    spread_back = (
        jnp.dot(image_low, pool_weight.T, preferred_element_type=jnp.float32) / counts[:, None]
    )
    slopes = [
        (
            bn_gain[k]
            * scales[k]
            * (grads[k] - rear[k, 0] / total - normed[k] * rear[k, 1] / total)
        ).astype(jnp.bfloat16)
        for k in range(4)
    ]
    input_grad = jnp.dot(slopes[0], point_weight.T, preferred_element_type=jnp.float32) + jnp.take(
        spread_back, local_ids, axis=0
    )
    point_part = jnp.einsum("pc,pf->cf", flat, slopes[0], preferred_element_type=jnp.float32)
    atrous_parts = []
    for branch in range(3):
        for tap in range(9):
            down, right = offsets(branch, tap)
            masked = slopes[branch + 1] * keeps[branch * 9 + tap].astype(jnp.bfloat16)
            atrous_parts.append(
                jnp.einsum(
                    "pc,pf->cf", shifted(down, right), masked, preferred_element_type=jnp.float32
                )
            )
    atrous_part = jnp.stack(atrous_parts).reshape(3, 3, 3, chans, feat)
    stacked = jnp.concatenate(slopes[1:], axis=1).reshape(rows, cols, 3 * feat)
    wide_slopes = lax.all_gather(stacked, "col", axis=1, tiled=True)
    tall_slopes = padded(wide_slopes, (("row", 0),), reach)
    slope_window = jnp.pad(tall_slopes, ((0, 0), (reach, reach), (0, 0)))
    for branch in range(3):
        for tap in range(9):
            down, right = offsets(branch, tap)
            source_row = reach - down
            source_col = reach - right + start_col
            far = lax.dynamic_slice(
                slope_window, (source_row, source_col, branch * feat), (rows, cols, feat)
            ).reshape(pixels, feat)
            far_marks = lax.dynamic_slice(
                window_marks, (source_row, source_col), (rows, cols)
            ).reshape(pixels, 1)
            keep = (far_marks == own_marks).astype(jnp.bfloat16)
            input_grad = input_grad + jnp.dot(
                far * keep,
                atrous_weight[branch, tap // 3, tap % 3].T,
                preferred_element_type=jnp.float32,
            )
    point_rows, atrous_rows = (
        lax.psum_scatter(point_part, "row", scatter_dimension=0, tiled=True),
        lax.psum_scatter(atrous_part, "row", scatter_dimension=3, tiled=True),
    )
    point_grad, atrous_grad = (
        lax.psum(point_rows.astype(jnp.bfloat16), "col").astype(jnp.float32),
        lax.psum(atrous_rows.astype(jnp.bfloat16), "col").astype(jnp.float32),
    )
    gain_grad = jnp.concatenate([rear[:, 1], head_back[1][None]], axis=0)
    shift_grad = jnp.concatenate([rear[:, 0], head_back[0][None]], axis=0)
    input_out = input_grad.astype(jnp.bfloat16).reshape(rows, cols, chans)
    return (
        output,
        input_out,
        point_grad,
        atrous_grad,
        pool_grad,
        project_grad,
        gain_grad,
        shift_grad,
    )


def solution(mesh):
    placed = (
        P("row", "col", None),
        P("row", "col"),
        P(),
        P(),
        P(),
        P(),
        P(),
        P(),
        P("row", "col", None),
    )
    return jax.shard_map(
        per_device,
        mesh=mesh,
        in_specs=placed,
        out_specs=(
            P("row", "col", None),
            P("row", "col", None),
            P("row", None),
            P(None, None, None, "row", None),
            P("row", None),
            P(),
            P(),
            P(),
        ),
        check_vma=False,
    )
```

profile of v0, /device:TPU:0, one launch (start us, length us, event | category | flops | bytes accessed | tf_op | source)
XLA Modules:
  0.0 1722.0 jit_solution(1701660915836287200)
XLA Ops:
  9.5 6.2 all_gather.9
  15.7 55.8 %all-gather.3.cloned.1.call-done = bf16[64,32,2048]{2,1,0:T(8,128)(2,1)} async-done(((bf16[64,8,2048]{2,1,0:T(8,128)(2,1)}), bf16[64,32,2048]{2,1,0:T(8,128)(2,1)}) %all-gather.3.cloned.1.call-update) | async-done | bytes 8388624 | tf_op jit(solution)/shard_map/all_gather | solution.py:63
  71.5 5.3 fusion.947
  94.1 89.1 %collective-permute-done = s32[18,32]{0,1:T(8,128)S(1)} collective-permute-done((s32[18,32]{0,1:T(8,128)S(1)}, s32[18,32]{0,1:T(8,128)S(1)}, u32[]{:S(2)}, u32[]{:S(2)}) %collective-permute-start) | collective-permute-done | bytes 2336 | tf_op jit(solution)/shard_map/ppermute | solution.py:20
  203.1 14.3 fusion.5
  296.0 41.5 %all-reduce.3 = (f32[17]{0:T(128)S(1)}, f32[4,2,256]{2,1,0:T(2,128)S(1)}) all-reduce(f32[17]{0:T(128)S(1)} %copy-done.99, f32[4,2,256]{2,1,0:T(2,128)S(1)} %pad_maximum_fusion), channel_id=1, replica_groups=mesh['row'=8,'col'=4] {'row','col'}, use_global_device_ids=true, to_apply=%region_10.11 | all-reduce | flops 2065 | bytes 16520 | tf_op jit(solution)/shard_map/psum | solution.py:107
  351.6 40.1 %psum.73 = f32[2,256]{1,0:T(2,128)S(1)} all-reduce(f32[2,256]{1,0:T(2,128)S(1)} %pad_maximum_fusion.4), channel_id=1, replica_groups=mesh['row'=8,'col'=4] {'row','col'}, use_global_device_ids=true, to_apply=%region_16.17 | all-reduce | flops 512 | bytes 4096 | tf_op jit(solution)/shard_map/psum | solution.py:122
  394.7 40.1 %psum.74 = f32[2,256]{1,0:T(2,128)S(1)} all-reduce(f32[2,256]{1,0:T(2,128)S(1)} %pad_maximum_fusion.5), channel_id=1, replica_groups=mesh['row'=8,'col'=4] {'row','col'}, use_global_device_ids=true, to_apply=%region_19.20 | all-reduce | flops 512 | bytes 4096 | tf_op jit(solution)/shard_map/psum | solution.py:129
  445.1 40.1 %psum.75 = f32[5,2,256]{2,0,1:T(8,128)S(1)} all-reduce(f32[5,2,256]{2,0,1:T(8,128)S(1)} %stack.271), channel_id=1, replica_groups=mesh['row'=8,'col'=4] {'row','col'}, use_global_device_ids=true, to_apply=%region_30.31 | all-reduce | flops 2560 | bytes 20480 | tf_op jit(solution)/shard_map/psum | solution.py:147
  496.0 5.0 fusion.38
  505.7 4.9 fusion.36
  510.7 4.9 fusion.35
  520.3 4.9 fusion.33
  535.0 4.9 fusion.30
  589.3 875.5 %reduce-scatter.5.cloned.1.call-done = f32[3,3,3,256,256]{4,3,2,1,0:T(8,128)} async-done(((f32[3,3,3,2048,256]{4,3,2,1,0:T(8,128)}), f32[3,3,3,256,256]{4,3,2,1,0:T(8,128)}) %reduce-scatter.5.cloned.1.call-update) | async-done | bytes 7077904 | tf_op jit(solution)/shard_map/reduce_scatter | solution.py:206
  1464.8 5.2 convert_element_type.924
  1487.5 40.6 %psum.76 = bf16[17,256]{1,0:T(8,128)(2,1)S(1)} all-reduce(f32[17,256]{1,0:T(8,128)} %fusion.506), channel_id=1, replica_groups=mesh['row'=8,'col'=4] {'row','col'}, use_global_device_ids=true, to_apply=%region_31.32 | all-reduce | flops 4352 | bytes 26112 | tf_op jit(solution)/shard_map/psum | solution.py:152
  1534.8 5.1 collective-permute-start.4
  1551.9 25.7 %collective-permute-done.4 = bf16[18,32,768]{2,1,0:T(8,128)(2,1)} collective-permute-done((bf16[18,32,768]{2,1,0:T(8,128)(2,1)S(1)}, bf16[18,32,768]{2,1,0:T(8,128)(2,1)}, u32[]{:S(2)}, u32[]{:S(2)}) %collective-permute-start.4) | collective-permute-done | bytes 884768 | tf_op jit(solution)/shard_map/ppermute | solution.py:20
  1577.6 6.1 fusion.11
  1583.8 5.2 fusion.338
  1589.0 5.1 fusion.365
  1665.7 38.7 %fusion.12 = bf16[64,8,2048]{2,1,0:T(8,128)(2,1)} fusion(f32[512,2048]{1,0:T(8,128)} %fusion.329, f32[512,2048]{1,0:T(8,128)} %fusion.332, f32[512,2048]{1,0:T(8,128)} %fusion.335, f32[512,2048]{1,0:T(8,128)} %fusion.338, f32[512,2048]{1,0:T(8,128)} %fusion.341, f32[512,2048]{1,0:T(8,128)} %fusion.344, f32[512,2048]{1,0:T(8,128)} %fusion.347, ...), kind=kOutput, calls=%fused_computation.19 | convolution fusion | flops 568852480 | bytes 120849920 | tf_op jit(solution)/shard_map/dot_general | solution.py:199
  1704.4 5.8 convert_element_type.925
  (577 shorter events, 334.3 us)
Async XLA Ops:
  8.1 63.4 %all-gather.3.cloned.1.call-start = ((), (), s32[]{:S(2)}) async-start(), calls=%async_computation.2 | async-start | bytes 10485760 | tf_op jit(solution)/shard_map/all_gather | solution.py:63
  8.8 328.7 %all-reduce.9.cloned.1.call-start = ((), (), s32[]{:S(2)}) async-start(), calls=%async_computation.3 | async-start | bytes 393216 | tf_op jit(solution)/shard_map/psum | solution.py:107
  76.7 126.3 %collective-permute-start.2 = (bf16[18,32,2048]{2,1,0:T(8,128)(2,1)}, bf16[18,32,2048]{2,1,0:T(8,128)(2,1)}, u32[]{:S(2)}, u32[]{:S(2)}) collective-permute-start(bf16[18,32,2048]{2,1,0:T(8,128)(2,1)} %get-tuple-element.119), channel_id=1, source_target_pairs={{0,4},{4,8},{8,12},{12,16},{16,20},{20,24},{24,28},{1,5},{5,9},{9,... | collective-permute-start | bytes 7077896 | tf_op jit(solution)/shard_map/ppermute | solution.py:20
  81.5 121.5 %collective-permute-start.3 = (bf16[18,32,2048]{2,1,0:T(8,128)(2,1)}, bf16[18,32,2048]{2,1,0:T(8,128)(2,1)}, u32[]{:S(2)}, u32[]{:S(2)}) collective-permute-start(bf16[18,32,2048]{2,1,0:T(8,128)(2,1)} %get-tuple-element.120), channel_id=1, source_target_pairs={{4,0},{8,4},{12,8},{16,12},{20,16},{24,20},{28,24},{5,1},{9,5},{13... | collective-permute-start | bytes 7077896 | tf_op jit(solution)/shard_map/ppermute | solution.py:21
  82.9 100.3 %collective-permute-start = (s32[18,32]{0,1:T(8,128)S(1)}, s32[18,32]{0,1:T(8,128)S(1)}, u32[]{:S(2)}, u32[]{:S(2)}) collective-permute-start(s32[18,32]{0,1:T(8,128)S(1)} %get-tuple-element.191), channel_id=1, source_target_pairs={{0,4},{4,8},{8,12},{12,16},{16,20},{20,24},{24,28},{1,5},{5,9},{9,... | collective-permute-start | bytes 6920 | tf_op jit(solution)/shard_map/ppermute | solution.py:20
  87.4 95.8 %collective-permute-start.1 = (s32[18,32]{0,1:T(8,128)S(1)}, s32[18,32]{0,1:T(8,128)S(1)}, u32[]{:S(2)}, u32[]{:S(2)}) collective-permute-start(s32[18,32]{0,1:T(8,128)S(1)} %get-tuple-element.192), channel_id=1, source_target_pairs={{4,0},{8,4},{12,8},{16,12},{20,16},{24,20},{28,24},{5,1},{9,5},{13... | collective-permute-start | bytes 6920 | tf_op jit(solution)/shard_map/ppermute | solution.py:21
  90.0 497.6 %reduce-scatter.3.cloned.1.call-start = ((), (), s32[]{:S(2)}) async-start(), calls=%async_computation.5 | async-start | bytes 2359296 | tf_op jit(solution)/shard_map/reduce_scatter | solution.py:205
  489.3 975.4 %reduce-scatter.5.cloned.1.call-start = ((), (), s32[]{:S(2)}) async-start(), calls=%async_computation.6 | async-start | bytes 63700992 | tf_op jit(solution)/shard_map/reduce_scatter | solution.py:206
  585.4 896.6 %copy-start.79 = (bf16[64,8]{0,1:T(8,128)(2,1)S(1)}, bf16[64,8]{0,1:T(8,128)(2,1)}, u32[]{:S(2)}) copy-start(bf16[64,8]{0,1:T(8,128)(2,1)} %get-tuple-element.157) | copy-start | bytes 3076
  585.4 896.6 %copy-start.78 = (bf16[64,8]{0,1:T(8,128)(2,1)S(1)}, bf16[64,8]{0,1:T(8,128)(2,1)}, u32[]{:S(2)}) copy-start(bf16[64,8]{0,1:T(8,128)(2,1)} %get-tuple-element.159) | copy-start | bytes 3076
  585.4 897.3 %copy-start.77 = (bf16[64,8]{0,1:T(8,128)(2,1)S(1)}, bf16[64,8]{0,1:T(8,128)(2,1)}, u32[]{:S(2)}) copy-start(bf16[64,8]{0,1:T(8,128)(2,1)} %get-tuple-element.161) | copy-start | bytes 3076
  585.4 897.4 %copy-start.76 = (bf16[64,8]{0,1:T(8,128)(2,1)S(1)}, bf16[64,8]{0,1:T(8,128)(2,1)}, u32[]{:S(2)}) copy-start(bf16[64,8]{0,1:T(8,128)(2,1)} %get-tuple-element.169) | copy-start | bytes 3076
  585.4 899.8 %copy-start.6 = (f32[512,256]{1,0:T(8,128)S(1)}, f32[512,256]{1,0:T(8,128)}, u32[]{:S(2)}) copy-start(f32[512,256]{1,0:T(8,128)} %gather_fusion) | copy-start | bytes 1572868
  585.4 899.8 %copy-start.35 = (s32[512]{0:T(512)S(1)}, s32[512]{0:T(512)}, u32[]{:S(2)}) copy-start(s32[512]{0:T(512)} %copy-done.34) | copy-start | bytes 6148
  585.5 899.8 %copy-start.57 = (f32[1,1,256]{2,1,0:T(1,128)S(1)}, f32[1,1,256]{2,1,0:T(1,128)}, u32[]{:S(2)}) copy-start(f32[1,1,256]{2,1,0:T(1,128)} %copy-done.56) | copy-start | bytes 3076
  585.5 899.8 %copy-start.59 = (f32[1,1,256]{2,1,0:T(1,128)S(1)}, f32[1,1,256]{2,1,0:T(1,128)}, u32[]{:S(2)}) copy-start(f32[1,1,256]{2,1,0:T(1,128)} %copy-done.58) | copy-start | bytes 3076
  585.5 899.8 %copy-start.61 = (pred[512]{0:T(512)(128)(4,1)S(1)}, pred[512]{0:T(512)(128)(4,1)}, u32[]{:S(2)}) copy-start(pred[512]{0:T(512)(128)(4,1)} %compare_and_fusion) | copy-start | bytes 1540
  585.5 943.2 %copy-start.9 = (bf16[2048,256]{1,0:T(8,128)(2,1)S(1)}, bf16[2048,256]{1,0:T(8,128)(2,1)}, u32[]{:S(2)}) copy-start(bf16[2048,256]{1,0:T(8,128)(2,1)} %param.13) | copy-start | bytes 3145732
  585.5 947.7 %all-gather.5.cloned.1.call-start = ((), (), s32[]{:S(2)}) async-start(), calls=%async_computation.4 | async-start | bytes 3932160 | tf_op jit(solution)/shard_map/all_gather | solution.py:184
  587.5 942.2 %copy-start.11 = (f32[512,256]{1,0:T(8,128)S(1)}, f32[512,256]{1,0:T(8,128)}, u32[]{:S(2)}) copy-start(f32[512,256]{1,0:T(8,128)} %get-tuple-element.231) | copy-start | bytes 1572868
  587.6 1116.8 %all-reduce.13.cloned.1.call-start = ((), (), s32[]{:S(2)}) async-start(), calls=%async_computation.8 | async-start | bytes 7340032 | tf_op jit(solution)/shard_map/psum | solution.py:209
  1470.0 241.9 %all-reduce.11.cloned.1.call-start = ((), (), s32[]{:S(2)}) async-start(), calls=%async_computation.7 | async-start | bytes 2621440 | tf_op jit(solution)/shard_map/psum | solution.py:147
  1534.8 42.8 %collective-permute-start.4 = (bf16[18,32,768]{2,1,0:T(8,128)(2,1)S(1)}, bf16[18,32,768]{2,1,0:T(8,128)(2,1)}, u32[]{:S(2)}, u32[]{:S(2)}) collective-permute-start(bf16[18,32,768]{2,1,0:T(8,128)(2,1)S(1)} %get-tuple-element.121), channel_id=1, source_target_pairs={{0,4},{4,8},{8,12},{12,16},{16,20},{20,24},{24,28},{1,5},{5,9},{9,... | collective-permute-start | bytes 2654216 | tf_op jit(solution)/shard_map/ppermute | solution.py:20
  1539.9 37.7 %collective-permute-start.5 = (bf16[18,32,768]{2,1,0:T(8,128)(2,1)S(1)}, bf16[18,32,768]{2,1,0:T(8,128)(2,1)}, u32[]{:S(2)}, u32[]{:S(2)}) collective-permute-start(bf16[18,32,768]{2,1,0:T(8,128)(2,1)S(1)} %get-tuple-element.122), channel_id=1, source_target_pairs={{4,0},{8,4},{12,8},{16,12},{20,16},{24,20},{28,24},{5,1},{9,5},{13... | collective-permute-start | bytes 2654216 | tf_op jit(solution)/shard_map/ppermute | solution.py:21
  (128 other events, 20119.7 us)
Sparse Core Ops, SparseCore 0:
  10.5 60.9 all-gather.2
  588.5 29.1 all-gather.4
  1470.1 77.6 all-reduce.12
  1554.0 131.5 all-reduce.10
Sparse Core Ops, SparseCore 1:
  90.1 158.0 all-reduce.8
  489.4 68.9 reduce-scatter.2
  585.3 879.4 reduce-scatter.4
where the time goes:
time: 1730 us; the launch traced here: 1720 us
  waiting for transfers between devices  1050 us (61%)
  matrix products  313 us (18%)
  blocking collectives  209 us (12%)
  other arithmetic  75.4 us (4%)
  local copies, waits for them, and re-layouts  41.7 us (2%)
  starting transfers between devices  19 us (1%)
  between operations  17.4 us (1%)
    reduce_scatter x1, waiting for transfers between devices, per_device(): lax.psum_scatter(atrous_part, 'row', scatter_dimension=3, tiled=True)  875 us
    dot_general x27, matrix products, per_device(): jnp.dot(far * keep, atrous_weight[branch, tap // 3, tap % 3].T, preferred...  120 us
    ppermute x3, waiting for transfers between devices, padded(): before = lax.ppermute(last, axis, up)  115 us
    dot_general x27, matrix products, per_device(): jnp.einsum('pc,pf->cf', shifted(down, right), masked, preferred_element_t...  93.1 us
    dot_general x27, matrix products, per_device(): jnp.dot(shifted(down, right), atrous_weight[branch, tap // 3, tap % 3], p...  77.7 us
    all_gather x1, waiting for transfers between devices, per_device(): lax.all_gather(feature_map, 'col', axis=1, tiled=True)  55.8 us
    psum x1, blocking collectives, per_device(): lax.psum((part_sums, part_counts, jnp.stack([moments(v) for v in branch_o...  41.5 us
    psum x1, blocking collectives, per_device(): image_slope = lax.psum(local_image, ('row', 'col'))  40.6 us
  transfers between devices with their start and end apart: 13, of which 4 were waited for; matrix products, arithmetic and copies ran while one was open for 23% of the time, Pallas kernels for 0%

commit v1 on v0

v1 whole, which is shorter than its diff:
```python
from functools import partial

import jax
import jax.numpy as jnp
from jax import lax
from jax.experimental import pallas as pl
from jax.experimental.pallas import tpu as pltpu
from jax.sharding import Mesh, PartitionSpec as P

REACH = 18
IMG_ROWS = 32
EPSILON = 1e-05
PAD = 32
SWAP = [(0, 1), (1, 0)]
BF = jnp.bfloat16
F32 = jnp.float32
VMEM_LIMIT = 60 * 2**20


def dot(a, b):
    return jnp.dot(a, b, preferred_element_type=F32)


def exact(a, b):
    return jnp.dot(a, b, precision=lax.Precision.HIGHEST, preferred_element_type=F32)


def swap(x, axis):
    return lax.ppermute(x, axis, SWAP)


def crossed(x):
    return lax.ppermute(x, ("y", "x"), [(i, 3 - i) for i in range(4)])


def quad(x, axes):
    near, far, last = (
        lax.ppermute(x, axes, [(i, i ^ step) for i in range(4)]) for step in (1, 2, 3)
    )
    return (x + near) + (far + last)


def z_sum(x):
    count = lax.axis_size("z")
    if count == 4:
        return quad(x, "z")
    step = 1
    while step < count:
        x = x + lax.ppermute(x, "z", [(i, i ^ step) for i in range(count)])
        step *= 2
    return x


def plane_sum(x):
    return quad(x, ("y", "x"))


def allsum(x):
    x = plane_sum(z_sum(x))
    return x + swap(x, "k")


def smooth(value):
    return jax.nn.gelu(value, approximate=True)


def smooth_slope(value):
    root = 0.7978845608028654
    square = value * value
    tanh = jnp.tanh(root * (value + 0.044715 * value * square))
    return 0.5 * (1.0 + tanh) + 0.5 * value * (1.0 - tanh * tanh) * root * (
        1.0 + 3 * 0.044715 * square
    )


def moments(value):
    return jnp.stack([jnp.sum(value, axis=0), jnp.sum(value * value, axis=0)])


def place_of(info, n):
    dk, dy, dx = n // 4, n // 2 % 2, n % 2
    col = ((info[1] ^ dx) * 2 + (info[2] ^ dk)) * 8
    return REACH + col, info[0] ^ dy


def tile_copies(info, tiles, window, sems, lane=0):
    width = window.shape[-1]
    copies = []
    for n, tile in enumerate(tiles):
        col, y = place_of(info, n)
        row = pl.multiple_of(PAD + y * 64, 16)
        copies.append(
            pltpu.make_async_copy(
                tile.at[:, pl.ds(0, 64), pl.ds(lane, width)],
                window.at[pl.ds(col, 8), pl.ds(row, 64)],
                sems.at[n],
            )
        )
        rim = tile.shape[1] - 64
        if rim:
            row = pl.multiple_of(jnp.where(y == 0, PAD + 128, PAD - rim), 16)
            copies.append(
                pltpu.make_async_copy(
                    tile.at[:, pl.ds(64, rim), pl.ds(lane, width)],
                    window.at[pl.ds(col, 8), pl.ds(row, rim)],
                    sems.at[8 + n],
                )
            )
    for copy in copies:
        copy.start()
    return copies


def place_rims(info, rims, window):
    for dk, rim in enumerate(rims):
        for n in range(4):
            col = REACH + ((n % 2) * 2 + (info[2] ^ dk)) * 8
            row = PAD + 128 if n < 2 else PAD - REACH
            for q in range(8):
                window[col + q, row : row + REACH, :] = rim[n, q]


def shift_rows(window, masks, b, q, i, spread, sign, cut, ok=None):
    start = PAD + sign * (i - 1) * spread
    value = window[REACH + q, start : start + 128, :]
    if i != 1:
        keep = masks[b, 1 if sign * (i - 1) > 0 else 0]
        keep = jnp.where(q >= cut, keep, jnp.ones_like(keep))
        if ok is not None:
            keep = jnp.where(ok, keep, jnp.zeros_like(keep))
        value = value * jnp.concatenate([keep] * (value.shape[1] // 128), axis=1)
    elif ok is not None:
        value = jnp.where(ok, value, jnp.zeros_like(value))
    return value


def tap_rows(window, masks, b, col, width, spread, sign, cut):
    return jnp.concatenate(
        [
            jnp.concatenate(
                [shift_rows(window, masks, b, col + u, i, spread, sign, cut) for i in range(3)],
                axis=1,
            )
            for u in range(width)
        ],
        axis=0,
    )


def branch_sum(window, masks, b, col, spread, sign, cut, product, acc, fresh):
    width = 2

    def inside(j, e):
        source = col + e + sign * (j - 1) * spread
        return (source >= 0) & (source < 32) & ((source < cut) == (col + e < cut))

    def center(e):
        return product(1, tap_rows(window, masks, b, col + e, width, spread, sign, cut))

    def side(j, e):
        source = col + e + sign * (j - 1) * spread
        part = product(j, tap_rows(window, masks, b, source, width, spread, sign, cut))
        return jnp.concatenate(
            [
                jnp.where(inside(j, e + u), part[u * 128 : u * 128 + 128], 0.0)
                for u in range(width)
            ],
            axis=0,
        )

    def put(e, value, first):
        value = value.reshape(width, 128, acc.shape[-1])
        if first:
            acc[e : e + width] = value
        else:
            acc[e : e + width] += value

    dense = spread == REACH // 3
    for e in range(0, 8, width):
        value = center(e)
        if dense:
            value = value + side(0, e) + side(2, e)
        put(e, value, fresh)
    if dense:
        return
    for j in (0, 2):
        some = inside(j, 0)
        for e in range(1, 8):
            some = some | inside(j, e)

        @pl.when(some)
        def _(j=j):
            for e in range(0, 8, width):
                put(e, side(j, e), False)


def forward_kernel(units, spreads, lanes, info, *refs):
    mains, rims = refs[:8], refs[8:10]
    masks, point, weights = refs[10:13]
    outs = refs[13:17]
    window, point_buf, weight_buf, acc, sems, weight_sems = refs[17:]
    iy, ix, ik, cut = info[0], info[1], info[2], info[3]
    copies = tile_copies(info, mains, window, sems)
    loads = []
    for n, b in enumerate(units):
        if b is None:
            loads.append(
                [pltpu.make_async_copy(point.at[:, iy, ix], point_buf, weight_sems.at[n, 0])]
            )
        else:
            loads.append(
                [
                    pltpu.make_async_copy(
                        weights.at[b, i, j, :, iy, ix],
                        weight_buf.at[n, j, i],
                        weight_sems.at[n, 3 * j + i],
                    )
                    for j in range(3)
                    for i in range(3)
                ]
            )
        for copy in loads[n]:
            copy.start()
    place_rims(info, rims, window)
    for copy in copies:
        copy.wait()
    for n, b in enumerate(units):
        for copy in loads[n]:
            copy.wait()
        keep, send = outs[2 * n : 2 * n + 2]
        for dx in (1, 0):
            col = (ix ^ dx) * 16 + ik * 8
            if b is None:
                source = window[pl.ds(REACH + col, 8), PAD : PAD + 128, :].reshape(1024, lanes)
                acc[...] = dot(source, point_buf[...].reshape(lanes, 256)).reshape(8, 128, 256)
            else:

                def product(j, rows, n=n):
                    return dot(rows, weight_buf[n, j].reshape(3 * lanes, 256))

                branch_sum(window, masks, b, col, spreads[b], 1, cut, product, acc, True)
            for dy in range(2):
                row = pl.multiple_of((iy ^ dy) * 64, 64)
                value = acc[:, pl.ds(row, 64), :]
                if (dy if n else dx) == 0:
                    keep[dx if n else dy] = value
                else:
                    send[dx if n else dy] = value.astype(BF)


def input_kernel(chosen, spreads, lanes, pointed, info, *refs):
    count = 8 * (1 + max(c[1] for c in chosen))
    tiles, masks, point, weights = refs[:count], refs[count], refs[count + 1], refs[count + 2]
    rest = refs[count + 3 :]
    if pointed:
        before, edge, strip = rest[:3]
        outs = rest[3:7]
        windows, weight_buf, point_buf, acc, sems, weight_sems = rest[7:]
    else:
        (result,) = rest[:1]
        windows, weight_buf, sems, weight_sems = rest[1:]
        acc = result
    iy, ix, ik, cut = info[0], info[1], info[2], info[3]
    mine = acc.shape[-1]
    fetches, loads = [], []
    for n, (b, first, lane) in enumerate(chosen):
        group = tiles[8 * first : 8 * first + 8]
        fetches.append(tile_copies(info, group, windows.at[n], sems.at[n], lane))
        if b is None:
            loads.append(
                [pltpu.make_async_copy(point.at[:, iy, ix], point_buf, weight_sems.at[n, 0])]
            )
        else:
            loads.append(
                [
                    pltpu.make_async_copy(
                        weights.at[b, i, j, :, iy, ix],
                        weight_buf.at[n, j, :, :, pl.ds(i * lanes, lanes)],
                        weight_sems.at[n, 3 * j + i],
                    )
                    for j in range(3)
                    for i in range(3)
                ]
            )
        for copy in loads[n]:
            copy.start()

    def times(a, w):
        return lax.dot_general(
            a, w.reshape(mine, w.shape[-1]), (((1,), (1,)), ((), ())), preferred_element_type=F32
        )

    for n, (b, _, _) in enumerate(chosen):
        for copy in fetches[n] + loads[n]:
            copy.wait()
        window = windows.at[n]
        for dx in range(2):
            col = (ix ^ dx) * 16 + ik * 8
            if b is None:
                for e in range(0, 8, 2):
                    source = window[pl.ds(REACH + col + e, 2), PAD : PAD + 128, :]
                    value = times(source.reshape(256, lanes), point_buf[...])
                    for u in range(2):
                        pool = jnp.where(col + e + u < cut, edge[...], strip[...])
                        acc[dx, e + u] += (
                            before[dx, e + u] + value[u * 128 : u * 128 + 128] + pool
                        )
            else:

                def product(j, rows, n=n):
                    return times(rows, weight_buf[n, j])

                branch_sum(
                    window, masks, b, col, spreads[b], -1, cut, product, acc.at[dx], n == 0
                )
    if pointed:
        for dx in range(2):
            for dy in range(2):
                row = pl.multiple_of((iy ^ dy) * 64, 64)
                outs[dy * 2 + dx][...] = acc[dx, :, pl.ds(row, 64), :].astype(BF)


def weight_kernel(spread, b, sources, lanes, info, *refs):
    tiles = refs[:8]
    masks, across = refs[8:10]
    outs = refs[10:-4]
    windows, out, sems, out_sems = refs[-4:]
    cut = info[3]
    parts = out.shape[0]
    each = out.shape[2]
    paired = len(outs) == 2
    fetches = [
        tile_copies(info, tiles, windows.at[n], sems.at[n], lane)
        for n, lane in enumerate(sources)
    ]

    def emit(t, value):
        for z in range(parts):
            out[info[4] ^ z if paired else z, t] = value[z * each : (z + 1) * each].astype(BF)

    for copy in fetches[0]:
        copy.wait()
    window = windows.at[0]
    for j in (1, 0, 2):
        move = (j - 1) * spread
        columns = [p for p in range(32) if 0 <= p + move < 32]
        total = None
        for at in range(0, len(columns), 8):
            group = columns[at : at + 8]
            right = []
            for p in group:
                ok = None if j == 1 else ((p < cut) == (p + move < cut))
                right.append(
                    jnp.concatenate(
                        [shift_rows(window, masks, b, p, i, spread, -1, cut, ok) for i in range(3)],
                        axis=1,
                    )
                )
            first, last = (group[0] + move) * 128, (group[-1] + move + 1) * 128
            part = dot(across[:, first:last], jnp.concatenate(right, axis=0))
            total = part if total is None else total + part
        for i in range(3):
            emit(3 * i + j, total[:, i * lanes : (i + 1) * lanes])
    if len(sources) > 1:
        for copy in fetches[1]:
            copy.wait()
        plain = windows[1, REACH : REACH + 32, PAD : PAD + 128, :].reshape(32 * 128, lanes)
        emit(9, dot(across[...], plain))
    if paired:
        moves = [(0, outs[0].at[0]), (3, outs[0].at[1]), (1, outs[1].at[0]), (2, outs[1].at[1])]
        moves = [(out.at[m], target) for m, target in moves]
    else:
        moves = [(out, outs[0])]
    copies = [
        pltpu.make_async_copy(source, target, out_sems.at[n])
        for n, (source, target) in enumerate(moves)
    ]
    for copy in copies:
        copy.start()
    for copy in copies:
        copy.wait()


def collect_kernel(first, count, extra, info, *refs):
    pieces = refs[:4]
    outs = refs[len(refs) - 3 - extra : len(refs) - 2]
    buf, sem = refs[len(refs) - 2 :]
    ix, ik = info[1], info[2]
    for n, piece in enumerate(pieces):
        index = (ix ^ (n // 2)) * 2 + (ik ^ (n % 2))
        for t in range(count):
            buf[t, index] = piece[t].astype(F32)
        for e in range(extra):
            outs[1 + e][index] = piece[count + e].astype(F32)
    copy = pltpu.make_async_copy(buf, outs[0].at[pl.ds(first, count)], sem)
    copy.start()
    copy.wait()


def pack_kernel(share, info, full, *refs):
    iy, ix = info[0], info[1]
    rims = refs[4]
    for n in range(4):
        other = (iy ^ (n // 2)) * 2 + (ix ^ (n % 2))
        for z in range(full.shape[-1] // (4 * share)):
            lane = pl.multiple_of((z * 4 + other) * share, 128)
            value = full[:, :, pl.ds(lane, share)]
            refs[n][:, :, z * share : (z + 1) * share] = value

            @pl.when(iy == 0)
            def _(value=value, other=other, z=z):
                rims[other, :, :, z * share : (z + 1) * share] = value[:, :REACH]

            @pl.when(iy == 1)
            def _(value=value, other=other, z=z):
                rims[other, :, :, z * share : (z + 1) * share] = value[:, 64 - REACH :]


def unpack_kernel(share, info, *refs):
    iy, ix = info[0], info[1]
    full = refs[4]
    for n in range(4):
        other = (iy ^ (n // 2)) * 2 + (ix ^ (n % 2))
        for z in range(full.shape[-1] // (4 * share)):
            lane = pl.multiple_of((z * 4 + other) * share, 128)
            full[:, :, pl.ds(lane, share)] = refs[n][:, :, z * share : (z + 1) * share]


def across_kernel(share, info, *refs):
    tiles, out, rows, zero = refs[:8], *refs[8:11]
    window, acc, sems = refs[11:]
    ik, cut = info[2], info[3]
    for copy in tile_copies(info, tiles, window, sems):
        copy.wait()
    acc[...] = jnp.zeros_like(acc)
    for q in range(32):
        value = window[REACH + q, PAD : PAD + 128, :]
        turned = value.T
        for z in range(turned.shape[0] // share):
            low = turned[z * share : z * share + share // 2]
            high = turned[z * share + share // 2 : (z + 1) * share]
            out[z * share // 2 : (z + 1) * share // 2, q * 128 : (q + 1) * 128] = jnp.where(
                ik == 0, low, high
            )
        acc[(q >= cut).astype(jnp.int32)] += value.astype(F32)
    rows[...] = acc[1]
    zero[...] = jnp.sum(acc[0], axis=0, keepdims=True)


VMEM = pl.BlockSpec(memory_space=pltpu.VMEM)
SMEM = pl.BlockSpec(memory_space=pltpu.SMEM)
ANY = pl.BlockSpec(memory_space=pl.ANY)


def call(kernel, name, flops, in_specs, out_shape, scratch, args, out_specs=None, aliases=None):
    return pl.pallas_call(
        kernel,
        name=name,
        in_specs=in_specs,
        out_specs=out_specs or jax.tree.map(lambda _: VMEM, out_shape),
        out_shape=out_shape,
        input_output_aliases=aliases or {},
        scratch_shapes=scratch,
        compiler_params=pltpu.CompilerParams(vmem_limit_bytes=VMEM_LIMIT),
        cost_estimate=pl.CostEstimate(flops=flops, bytes_accessed=10**7, transcendentals=0),
    )(*args)


def per_device(
    feature_map,
    image_ids,
    point_weight,
    atrous_weight,
    pool_weight,
    project_weight,
    bn_gain,
    bn_shift,
    out_grad,
):
    rows, cols, chans = feature_map.shape
    feat = point_weight.shape[1]
    pixels = rows * cols
    zs = lax.axis_size("z")
    axes = ("k", "x", "y", "z")
    iz, iy, ix, ik = (lax.axis_index(a) for a in ("z", "y", "x", "k"))
    row_count = 2 * zs
    total = float(pixels * row_count * 4)
    images = rows * row_count // IMG_ROWS + 1
    share = chans // (4 * zs)
    mine = chans // 4
    spreads = [REACH * (b + 1) // 3 for b in range(3)]
    def pick(first, second, index):
        return jnp.where(index == 0, first, second)

    def rim(x, depth):
        return pick(x[:, :depth], x[:, rows - depth :], iy)

    def beyond(x, dy, dx):
        pairs = []
        for z in range(zs):
            for y in range(2):
                far = z - 1 + 2 * y
                if 0 <= far < zs:
                    for i in range(2):
                        target = (far * 2 + (y ^ dy)) * 2 + (i ^ dx)
                        pairs.append(((z * 2 + y) * 2 + i, target))
        return lax.ppermute(x, ("z", "y", "x"), pairs)

    with jax.named_scope("marks"):
        strip_own = jnp.max(image_ids, axis=1)
        zero_own = jnp.sum((image_ids[0] == 0).astype(jnp.int32))
        both = jnp.concatenate([strip_own, zero_own[None]])
        others = [
            lax.ppermute(both, ("x", "k"), [(i, i ^ step) for i in range(4)]) for step in (1, 2, 3)
        ]
        for other in others:
            strip_own = jnp.maximum(strip_own, other[:rows])
            zero_own = zero_own + other[rows]
        cut = zero_own
    places = jnp.stack([iy, ix, ik, ik, iz]).astype(jnp.int32)
    turned = feature_map.transpose(1, 0, 2)
    aligned = share % 128 == 0
    with jax.named_scope("spread_features"):
        if aligned:
            tile_shape = jax.ShapeDtypeStruct((cols, rows, mine), BF)
            *tiles, brims = call(
                partial(pack_kernel, share),
                "pack",
                0,
                [SMEM, VMEM],
                [tile_shape] * 4 + [jax.ShapeDtypeStruct((4, cols, REACH, mine), BF)],
                [],
                [places, turned],
            )
        else:
            packed = turned.reshape(cols, rows, zs, 2, 2, share).transpose(3, 4, 0, 1, 2, 5)
            packed = packed.reshape(4, cols, rows, mine)
            tiles = [
                lax.dynamic_index_in_dim(packed, (iy ^ dy) * 2 + (ix ^ dx), 0, False)
                for dy in range(2)
                for dx in range(2)
            ]
            brims = pick(packed[:, :, :REACH], packed[:, :, rows - REACH :], iy)
        halo = lax.all_to_all(beyond(brims, 0, 0), ("y", "x"), 0, 0)
        halos = [halo, swap(halo, "k")]
        own, to_x, to_y, to_d = tiles
        mains = [own, swap(to_x, "x"), swap(to_y, "y"), crossed(to_d)]

    with jax.named_scope("marks"):
        strip_own, mains[1] = lax.optimization_barrier((strip_own, mains[1]))
        edge_own = pick(strip_own[:REACH], strip_own[rows - REACH :], iy)
        edge, cross = beyond(edge_own, 0, 0), beyond(edge_own, 1, 0)
        other = swap(strip_own, "y")
    mains = mains + [swap(g, "k") for g in mains]
    with jax.named_scope("marks"):
        strip_plane = jnp.concatenate([pick(strip_own, other, iy), pick(other, strip_own, iy)])
        top, bottom = pick(cross, edge, iy), pick(edge, cross, iy)
        strip_tall = jnp.concatenate([top, strip_plane, bottom])
        masks = jnp.stack(
            [
                jnp.stack(
                    [
                        strip_plane
                        == lax.slice_in_dim(strip_tall, REACH + s * d, REACH + s * d + 2 * rows)
                        for s in (-1, 1)
                    ]
                )
                for d in spreads
            ]
        )
        masks = jnp.broadcast_to(masks[..., None], (3, 2, 2 * rows, 128)).astype(BF)
        info = jnp.stack([iy, ix, ik, cut, iz]).astype(jnp.int32)


    local_ids = image_ids.T.reshape(pixels)
    image_range = jnp.arange(images, dtype=jnp.int32)
    table = local_ids[:, None] == image_range[None, :]

    point_view = point_weight.reshape(zs, 2, 2, share, feat)
    atrous_view = atrous_weight.reshape(3, 3, 3, zs, 2, 2, share, feat)

    def forward(units):
        shape = (2, cols, rows, feat)
        return call(
            partial(forward_kernel, units, spreads, mine),
            "forward_taps",
            2 * 2048 * mine * 256 * 15,
            [SMEM] + [ANY] * 8 + [VMEM] * 3 + [ANY] * 2,
            [jax.ShapeDtypeStruct(shape, F32), jax.ShapeDtypeStruct(shape, BF)] * 2,
            [
                pltpu.VMEM((32 + 2 * REACH, 2 * PAD + 128, mine), BF),
                pltpu.VMEM((zs, share, feat), BF),
                pltpu.VMEM((2, 3, 3, zs, share, feat), BF),
                pltpu.VMEM((8, 128, feat), F32),
                pltpu.SemaphoreType.DMA((16,)),
                pltpu.SemaphoreType.DMA((2, 9)),
            ],
            [info, *mains, *halos, masks, point_view, atrous_view],
        )

    def reduce_first(parts):
        keep_x, send_x, keep_y, send_y = parts
        return keep_x, swap(send_x, "x"), keep_y, swap(send_y, "y")

    def reduce_middle(parts):
        keep_x, got_x, keep_y, got_y = parts
        more_x = (keep_x[1] + got_x[1].astype(F32)).astype(BF)
        more_y = (keep_y[1] + got_y[1].astype(F32)).astype(BF)
        return more_x, more_y

    def reduce_last(parts, last_x, last_y):
        keep_x, got_x, keep_y, got_y = parts
        value_x = keep_x[0] + got_x[0].astype(F32) + last_x.astype(F32)
        value_y = keep_y[0] + got_y[0].astype(F32) + last_y.astype(F32)
        return [value_x.reshape(pixels, feat), value_y.reshape(pixels, feat)]

    early = forward([None, 0])
    early_got = reduce_first(early)
    late = forward([1, 2])
    early_got, late = lax.optimization_barrier((early_got, late))
    late_got = reduce_first(late)
    early_more = reduce_middle(early_got)
    early_last = [swap(early_more[0], "y"), swap(early_more[1], "x")]

    half = share // 2
    strip_table = strip_plane[:, None] == image_range[None, :]
    with jax.named_scope("across"):
        mains_late, early_last = lax.optimization_barrier((mains, early_last))
        if aligned:
            across, row_sums, zero_sums = call(
                partial(across_kernel, share),
                "across",
                2 * 10**9,
                [SMEM] + [ANY] * 8,
                [
                    jax.ShapeDtypeStruct((mine // 2, 32 * 2 * rows), BF),
                    jax.ShapeDtypeStruct((2 * rows, mine), F32),
                    jax.ShapeDtypeStruct((1, mine), F32),
                ],
                [
                    pltpu.VMEM((32 + 2 * REACH, 2 * PAD + 128, mine), BF),
                    pltpu.VMEM((2, 2 * rows, mine), F32),
                    pltpu.SemaphoreType.DMA((16,)),
                ],
                [info, *mains_late],
            )
        else:
            columns = []
            for x in range(2):
                for k in range(2):
                    index = [(ik ^ k) * 4 + (iy ^ y) * 2 + (ix ^ x) for y in range(2)]
                    stack = [lax.select_n(n.astype(jnp.int32), *mains_late) for n in index]
                    columns.append(jnp.concatenate(stack, axis=1))
            plane = jnp.concatenate(columns, axis=0)
            in_strip = (jnp.arange(32) >= cut)[:, None, None]
            row_sums = jnp.sum(jnp.where(in_strip, plane.astype(F32), 0.0), axis=0)
            zero_sums = jnp.sum(jnp.where(in_strip, 0.0, plane.astype(F32)), axis=(0, 1))[None]
            plane = plane.reshape(32, 2 * rows, zs, 2, half)
            plane = lax.dynamic_index_in_dim(plane, ik, 3, False)
            across = plane.reshape(32 * 2 * rows, mine // 2).T

    with jax.named_scope("image_sums"):
        sums = lax.dot_general(
            strip_table.astype(F32),
            row_sums,
            (((0,), (0,)), ((), ())),
            precision=lax.Precision.HIGHEST,
        )
        sums = jnp.where(image_range[:, None] == 0, zero_sums, sums)
        strip_rows = jnp.sum(strip_table.astype(F32), axis=0)
        tall = jnp.concatenate(
            [sums, jnp.broadcast_to(strip_rows[:, None], (images, 128))], axis=1
        )
        tall = z_sum(tall)
        image_sums = tall[:, :mine]
        whole = 4 * cols
        counts = jnp.where(
            image_range == 0,
            (cut * (rows * row_count)).astype(F32),
            tall[:, mine] * (whole - cut).astype(F32),
        )
        pooled = (image_sums / counts[:, None]).astype(BF)
        pool_mine = pool_weight.reshape(zs, 2, 2, share, feat)
        pool_mine = lax.dynamic_slice(
            pool_mine, (0, iy, ix, 0, 0), (zs, 1, 1, share, feat)
        ).reshape(mine, feat)
        per_image = plane_sum(dot(pooled, pool_mine))

    late_got, across = lax.optimization_barrier((late_got, across))
    late_more = reduce_middle(late_got)
    branches = reduce_last(early_got, *early_last)
    branches += reduce_last(late_got, swap(late_more[0], "y"), swap(late_more[1], "x"))

    moments_mine = jnp.concatenate([moments(value) for value in branches], axis=1)
    first = allsum(moments_mine)
    weighted = counts[:, None] * per_image
    pool_stats = jnp.stack([jnp.sum(weighted, axis=0), jnp.sum(weighted * per_image, axis=0)])
    four = 4 * feat
    flat_gain, flat_shift = bn_gain[:4].reshape(four), bn_shift[:4].reshape(four)
    mean = first[0] / total
    scale = lax.rsqrt(first[1] / total - mean * mean + EPSILON)
    normed = (jnp.concatenate(branches, axis=1) - mean) * scale
    lifted = normed * flat_gain + flat_shift
    mean4 = pool_stats[0] / total
    scale4 = lax.rsqrt(pool_stats[1] / total - mean4 * mean4 + EPSILON)
    normed4 = (per_image - mean4) * scale4
    lifted4 = normed4 * bn_gain[4] + bn_shift[4]
    joined = smooth(lifted).astype(BF)
    joined4 = smooth(lifted4).astype(BF)
    table_float = table.astype(F32)
    head = dot(joined, project_weight[:four]) + exact(
        table_float, dot(joined4, project_weight[four:])
    )
    head_stats = allsum(moments(head))
    head_mean = head_stats[0] / total
    head_scale = lax.rsqrt(head_stats[1] / total - head_mean * head_mean + EPSILON)
    head_norm = (head - head_mean) * head_scale
    head_lift = head_norm * bn_gain[5] + bn_shift[5]
    output = smooth(head_lift).astype(BF).reshape(cols, rows, feat).transpose(1, 0, 2)
    cotangent = out_grad.transpose(1, 0, 2).reshape(pixels, feat).astype(F32)
    head_grad = cotangent * smooth_slope(head_lift)
    head_back = allsum(
        jnp.stack([jnp.sum(head_grad, axis=0), jnp.sum(head_grad * head_norm, axis=0)])
    )
    head_slope = (
        bn_gain[5]
        * head_scale
        * (head_grad - head_back[0] / total - head_norm * head_back[1] / total)
    ).astype(BF)
    joined_grad = lax.dot_general(
        head_slope, project_weight[:four], (((1,), (1,)), ((), ())), preferred_element_type=F32
    )
    grads = joined_grad * smooth_slope(lifted)
    image_heads = jnp.einsum(
        "pi,pf->if", table.astype(BF), head_slope, preferred_element_type=F32
    )
    rear = jnp.concatenate(
        [
            jnp.stack([jnp.sum(grads, axis=0), jnp.sum(grads * normed, axis=0)]).reshape(8, feat),
            image_heads,
        ],
        axis=0,
    )
    rear = allsum(rear)
    shift_back, gain_back = rear[:4].reshape(four), rear[4:8].reshape(four)
    slopes = (
        flat_gain * scale * (grads - shift_back / total - normed * gain_back / total)
    ).astype(BF)

    with jax.named_scope("project_grad"):
        project_part = lax.dot_general(
            joined, head_slope, (((0,), (0,)), ((), ())), preferred_element_type=F32
        )

    with jax.named_scope("spread_slopes"):
        tiles_out = [
            slopes[:, first * feat : last * feat].reshape(cols, rows, -1)
            for first, last in ((3, 4), (2, 3), (0, 2))
        ]
        brim = beyond(rim(tiles_out[0], 32), 0, 0)
        brims = beyond(
            jnp.concatenate([rim(tiles_out[1], 16), rim(tiles_out[2], 16)], axis=2), 0, 0
        )
        def both_cores(got):
            return got + [swap(g, "k") for g in got]

        tile3 = jnp.concatenate([tiles_out[0], brim], axis=1)
        tile2 = jnp.concatenate([tiles_out[1], brims[:, :, :feat]], axis=1)
        tile1 = jnp.concatenate([tiles_out[2], brims[:, :, feat:]], axis=1)
        blocks = project_part.astype(BF).reshape(8, four // 8, feat)
        blocks, tile3 = lax.optimization_barrier((blocks, tile3))
        blocks = lax.all_to_all(blocks, ("y", "x", "k"), 0, 0)
        group3 = both_cores([tile3, swap(tile3, "x"), swap(tile3, "y"), crossed(tile3)])
        tile2, group3 = lax.optimization_barrier((tile2, group3))
        arrived2 = [tile2, swap(tile2, "x"), swap(tile2, "y"), crossed(tile2)]

    image_heads = rear[8:]
    grads4 = smooth_slope(lifted4) * exact(image_heads, project_weight[four:].astype(F32).T)
    shift4, gain4 = jnp.sum(grads4, axis=0), jnp.sum(grads4 * normed4, axis=0)
    image_slope = (
        bn_gain[4]
        * scale4
        * (grads4 - counts[:, None] * (shift4 / total + normed4 * gain4 / total))
    )
    image_low = image_slope.astype(BF)
    spread_back = (
        lax.dot_general(
            image_low, pool_mine, (((1,), (1,)), ((), ())), preferred_element_type=F32
        )
        / counts[:, None]
    )
    strip_back = exact(strip_table.astype(F32), spread_back)
    pooled_mine = lax.dynamic_slice_in_dim(pooled, iz * share + ik * half, half, 1)
    pool_part = jnp.einsum("ic,if->cf", pooled_mine, image_low, preferred_element_type=F32)

    def weight_grad(b, tiles, lanes_at):
        taps = 8 + len(lanes_at)
        return call(
            partial(weight_kernel, spreads[b], b, lanes_at, feat),
            "weight_taps",
            2 * 4096 * (mine // 2) * 256 * 15,
            [SMEM] + [ANY] * 8 + [VMEM] * 2,
            [jax.ShapeDtypeStruct((2, taps, half, feat), BF)] * 2
            if zs == 4
            else [jax.ShapeDtypeStruct((zs, taps, half, feat), BF)],
            [
                pltpu.VMEM((len(lanes_at), 32 + 2 * REACH, 2 * PAD + 128, feat), BF),
                pltpu.VMEM((zs, taps, half, feat), BF),
                pltpu.SemaphoreType.DMA((2, 16)),
                pltpu.SemaphoreType.DMA((4,)),
            ],
            [info, *tiles, masks, across],
            out_specs=[ANY] * (2 if zs == 4 else 1),
        )

    def z_scatter(part, behind):
        if zs != 4:
            return lax.psum_scatter(part[0], "z", scatter_dimension=0, tiled=True)[0].astype(F32)
        keep, send = part
        got = lax.ppermute(send, "z", [(i, i ^ 1) for i in range(4)])
        got, _ = lax.optimization_barrier((got, behind))
        more = (keep[1].astype(F32) + got[1].astype(F32)).astype(BF)
        last = lax.ppermute(more, "z", [(i, i ^ 3) for i in range(4)])
        return keep[0].astype(F32) + got[0].astype(F32) + last.astype(F32)

    def collect(part, first, extra, buffer, behind):
        done = z_scatter(part, behind)
        if extra is not None:
            done = jnp.concatenate([done, extra[None]], axis=0)
        done = done.astype(BF)
        from_x = swap(done, "x")
        pieces = [done, swap(done, "k"), from_x, swap(from_x, "k")]
        more = done.shape[0] - 9
        grad = jax.ShapeDtypeStruct((27, 4, half, feat), F32)
        side = jax.ShapeDtypeStruct((4, half, feat), F32)
        return call(
            partial(collect_kernel, first, 9, more),
            "collect",
            0,
            [SMEM] + [VMEM] * 4 + [ANY] * len(buffer),
            [grad] + [side] * more,
            [pltpu.VMEM((9, 4, half, feat), F32), pltpu.SemaphoreType.DMA],
            [places, *pieces, *buffer],
            out_specs=[ANY] + [VMEM] * more,
            aliases={5: 0} if buffer else {},
        )

    part3 = weight_grad(2, group3, [0])
    arrived2, part3 = lax.optimization_barrier((arrived2, part3))
    group2 = both_cores(arrived2)
    tile1, group2 = lax.optimization_barrier((tile1, group2))
    from_x, from_y = swap(tile1, "x"), swap(tile1, "y")
    part2 = weight_grad(1, group2, [0])
    from_x, from_y, part2 = lax.optimization_barrier((from_x, from_y, part2))
    cross_x = swap(from_y[: cols // 2], "x")
    cross_y = swap(from_x[cols // 2 :], "y")
    group2, part2 = lax.optimization_barrier((group2, part2))

    def input_part(chosen, groups, pointed, more, outs):
        n = len(chosen)
        scratch = [
            pltpu.VMEM((n, 32 + 2 * REACH, 2 * PAD + 128, feat), BF),
            pltpu.VMEM((n, 3, zs, share, 3 * feat), BF),
        ]
        if pointed:
            scratch += [pltpu.VMEM((zs, share, feat), BF), pltpu.VMEM((2, 8, 128, mine), F32)]
        scratch += [pltpu.SemaphoreType.DMA((n, 16)), pltpu.SemaphoreType.DMA((n, 9))]
        return call(
            partial(input_kernel, chosen, spreads, feat, pointed),
            "input_taps",
            2 * 2048 * mine * 256 * 20,
            [SMEM] + [ANY] * 8 * len(groups) + [VMEM] + [ANY] * 2 + [VMEM] * len(more),
            outs,
            scratch,
            [info, *[t for g in groups for t in g], masks, point_view, atrous_view, *more],
        )

    with jax.named_scope("input_grad"):
        sums_so_far = input_part(
            [(2, 0, 0), (1, 1, 0)],
            [group3, group2],
            False,
            [],
            jax.ShapeDtypeStruct((2, cols, 2 * rows, mine), F32),
        )
    cross_x, cross_y, sums_so_far = lax.optimization_barrier((cross_x, cross_y, sums_so_far))
    group1 = both_cores([tile1, from_x, from_y, jnp.concatenate([cross_x, cross_y], axis=0)])
    part1 = weight_grad(0, group1, [feat, 0])
    with jax.named_scope("input_grad"):
        group1, part1 = lax.optimization_barrier((group1, part1))
        shape = jax.ShapeDtypeStruct((cols, rows, mine), BF)
        own, to_x, to_y, to_d = input_part(
            [(0, 0, feat), (None, 0, 0)],
            [group1],
            True,
            [sums_so_far, spread_back[:1], strip_back],
            [shape] * 4,
        )
        got = [own, swap(to_x, "x"), swap(to_y, "y"), crossed(to_d)]
        if aligned:
            input_turned = call(
                partial(unpack_kernel, share),
                "unpack",
                0,
                [SMEM] + [VMEM] * 4,
                jax.ShapeDtypeStruct((cols, rows, chans), BF),
                [],
                [places, *got],
            )
        else:
            planes = []
            for y in range(2):
                for x in range(2):
                    index = ((iy ^ y) * 2 + (ix ^ x)).astype(jnp.int32)
                    planes.append(lax.select_n(index, *got).reshape(cols, rows, zs, share))
            input_turned = jnp.stack(planes, axis=3).reshape(cols, rows, chans)
        input_grad = input_turned.transpose(1, 0, 2)

    with jax.named_scope("project_grad"):
        blocks, _ = lax.optimization_barrier((blocks, part3))
        project_sum = z_sum(jnp.sum(blocks.astype(F32), axis=0)).astype(BF)
        project_sum, _ = lax.optimization_barrier((project_sum, sums_so_far))
        project_sum = lax.all_to_all(
            jnp.broadcast_to(project_sum[None], (8, four // 8, feat)), ("y", "x", "k"), 0, 0
        ).reshape(four, feat)
        project_pool = lax.dot_general(
            joined4.astype(F32),
            image_heads,
            (((0,), (0,)), ((), ())),
            precision=lax.Precision.HIGHEST,
        )
        project_grad = jnp.concatenate([project_sum.astype(F32), project_pool], axis=0)

    (grad,) = collect(part3, 18, None, [], part2)
    (grad,) = collect(part2, 9, None, [grad], sums_so_far)
    grad, point_grad, pool_grad = collect(part1, 0, pool_part, [grad], own)
    atrous_grad = grad.reshape(3, 3, 3, 4 * half, feat)
    point_grad, pool_grad = (v.reshape(4 * half, feat) for v in (point_grad, pool_grad))

    gain_grad = jnp.concatenate([rear[4:8], gain4[None], head_back[1][None]], axis=0)
    shift_grad = jnp.concatenate([rear[:4], shift4[None], head_back[0][None]], axis=0)
    return (
        output,
        input_grad,
        point_grad,
        atrous_grad,
        pool_grad,
        project_grad,
        gain_grad,
        shift_grad,
    )


def solution(mesh):
    row, col = mesh.devices.shape
    fine = Mesh(mesh.devices.reshape(row // 2, 2, col // 2, 2), ("z", "y", "x", "k"))
    rows, cols = ("z", "y"), ("x", "k")
    placed = (
        P(rows, cols, None),
        P(rows, cols),
        P(),
        P(),
        P(),
        P(),
        P(),
        P(),
        P(rows, cols, None),
    )
    return jax.shard_map(
        per_device,
        mesh=fine,
        in_specs=placed,
        out_specs=(
            P(rows, cols, None),
            P(rows, cols, None),
            P(rows, None),
            P(None, None, None, rows, None),
            P(rows, None),
            P(),
            P(),
            P(),
        ),
        check_vma=False,
    )
```

time: 1730 us -> 427 us (0.25)
  waiting for transfers between devices: 1050 us -> 134 us
  matrix products: 313 us -> 11.8 us
  blocking collectives: 209 us -> 0 us
  Pallas kernels: 0 us -> 114 us
  starting transfers between devices: 19 us -> 107 us
  other arithmetic: 75.4 us -> 21.9 us
    reduce_scatter x2 -> x0, waiting for transfers between devices: 875 us -> none  [the longest x1 875 us: per_device(): lax.psum_scatter(atrous_part, 'row', scatter_dimension=3, tiled=True)]
    dot_general x92 -> x13, matrix products: 313 us -> 11.8 us  [the longest x1 3.59 us: per_device(): lax.dot_general(joined, head_slope, (((0,), (0,)), ((), ())), preferred_e...]
    psum x5 -> x0, blocking collectives: 203 us -> none  [the longest x1 41.5 us: per_device(): lax.psum((part_sums, part_counts, jnp.stack([moments(v) for v in branch_o...]
    pallas_call x0 -> x13, Pallas kernels: none -> 114 us  [call(): pl.pallas_call(kernel, name=name, in_specs=in_specs, out_specs=out_specs...]
    ppermute x6 -> x102, starting transfers between devices: 18.3 us -> 96.3 us  [the longest x33 40.8 us: quad(): lax.ppermute(x, axes, [(i, i ^ step) for i in range(4)])]
    all_gather x2 -> x0, waiting for transfers between devices: 55.8 us -> none  [the longest x1 55.8 us: per_device(): lax.all_gather(feature_map, 'col', axis=1, tiled=True)]
    convert_element_type x59 -> x17, other arithmetic: 31.6 us -> 8.62 us  [the longest x2 2.24 us: collect(): done = done.astype(BF)]
    concatenate x6 -> x13, other arithmetic: 23.8 us -> 3.39 us  [the longest x1 1.14 us: per_device(): jnp.concatenate([project_sum.astype(F32), project_pool], axis=0)]
  transfers between devices with their start and end apart: 13 -> 105, of which waited for: 4 -> 50; matrix products, arithmetic and copies ran while one was open for 23% -> 10% of each run, Pallas kernels for 0% -> 23%
where the time goes in v1:
time: 427 us; the launch traced here: 422 us
  waiting for transfers between devices  134 us (31%)
  Pallas kernels  114 us (27%)
  starting transfers between devices  107 us (25%)
  local copies, waits for them, and re-layouts  27.2 us (6%)
  other arithmetic  21.9 us (5%)
  matrix products  11.8 us (3%)
  between operations  5.01 us (1%)
    pallas_call x13, Pallas kernels, call(): pl.pallas_call(kernel, name=name, in_specs=in_specs, out_specs=out_specs...  114 us
    ppermute x51, waiting for transfers between devices, swap(): return lax.ppermute(x, axis, SWAP)  49.6 us
    ppermute x33, starting transfers between devices, quad(): lax.ppermute(x, axes, [(i, i ^ step) for i in range(4)])  40.8 us
    ppermute x51, starting transfers between devices, swap(): return lax.ppermute(x, axis, SWAP)  35.8 us
    ppermute x33, waiting for transfers between devices, quad(): lax.ppermute(x, axes, [(i, i ^ step) for i in range(4)])  30.4 us
    ppermute x4, waiting for transfers between devices, crossed(): return lax.ppermute(x, ('y', 'x'), [(i, 3 - i) for i in range(4)])  22.5 us
    ppermute x5, waiting for transfers between devices, beyond(): return lax.ppermute(x, ('z', 'y', 'x'), pairs)  15.1 us
    unnamed x170, local copies, waits for them, and re-layouts  13 us
  transfers between devices with their start and end apart: 105, of which 50 were waited for; matrix products, arithmetic and copies ran while one was open for 10% of the time, Pallas kernels for 23%

profile of v1, /device:TPU:0, one launch (start us, length us, event | category | flops | bytes accessed | tf_op | source)
XLA Modules:
  0.0 422.0 jit_solution(18237544913004926636)
XLA Ops:
  6.5 4.1 copy.52
  11.3 3.8 pack.1
  32.1 6.3 %collective-permute-done.14 = s32[18]{0:T(128)S(1)} collective-permute-done((s32[18]{0:T(128)S(1)}, s32[18]{0:T(128)S(1)}, u32[]{:S(2)}, u32[]{:S(2)}) %collective-permute-start.14) | collective-permute-done | bytes 104 | tf_op jit(solution)/shard_map/marks/ppermute | solution.py:507
  47.4 9.3 %all-to-all-done = bf16[4,8,18,512]{3,1,2,0:T(8,128)(2,1)S(1)} async-done(((bf16[4,8,18,512]{3,1,2,0:T(8,128)(2,1)}), bf16[4,8,18,512]{3,1,2,0:T(8,128)(2,1)S(1)}, u32[]{:S(2)}, u32[]{:S(2)}) %all-to-all-start) | async-done | bytes 589856 | tf_op jit(solution)/shard_map/spread_features/all_to_all | solution.py:544
  60.6 11.7 %forward_taps.2 = (f32[2,8,64,256]{3,2,1,0:T(8,128)}, bf16[2,8,64,256]{3,2,1,0:T(8,128)(2,1)}, f32[2,8,64,256]{3,2,1,0:T(8,128)}, bf16[2,8,64,256]{3,2,1,0:T(8,128)(2,1)}) custom-call(s32[5]{0:T(128)} %stack.133.info, bf16[8,64,512]{2,1,0:T(8,128)(2,1)} %get-tuple-element.145.refs_0_, bf16[8,64,512]{2,1,0:T(8,128)(2,1)} %copy-done.2, ...), custom_call_target="tpu_custom_call" | custom-call | flops 8053063680 | bytes 10000000 | tf_op jit(solution)/shard_map/forward_taps/pallas_call | solution.py:456
  74.4 19.5 %forward_taps.3 = (f32[2,8,64,256]{3,2,1,0:T(8,128)}, bf16[2,8,64,256]{3,2,1,0:T(8,128)(2,1)}, f32[2,8,64,256]{3,2,1,0:T(8,128)}, bf16[2,8,64,256]{3,2,1,0:T(8,128)(2,1)}) custom-call(s32[5]{0:T(128)} %stack.133.info, bf16[8,64,512]{2,1,0:T(8,128)(2,1)} %get-tuple-element.145.refs_0_, bf16[8,64,512]{2,1,0:T(8,128)(2,1)} %copy-done.2, ...), custom_call_target="tpu_custom_call" | custom-call | flops 8053063680 | bytes 10000000 | tf_op jit(solution)/shard_map/forward_taps/pallas_call | solution.py:456
  106.6 5.8 %across.1 = (bf16[256,4096]{1,0:T(8,128)(2,1)}, f32[128,512]{1,0:T(8,128)}, f32[1,512]{1,0:T(1,128)}) custom-call(s32[5]{0:T(128)} %stack.133.info, bf16[8,64,512]{2,1,0:T(8,128)(2,1)} %get-tuple-element.145.refs_0_, bf16[8,64,512]{2,1,0:T(8,128)(2,1)} %copy-done.2, bf16[8,64,512]{2,1,0:T(8,128)(2,1)} %copy-done.3, bf16[8,64,512]{2,1,0:T(8,128)(2,1)} %copy-done.4, ...), custom_call_target="tpu_custom_call" | custom-call | flops 2000000000 | bytes 10000000 | tf_op jit(solution)/shard_map/across/across/pallas_call | solution.py:456
  207.2 6.4 %collective-permute-done.58 = bf16[8,32,256]{2,1,0:T(8,128)(2,1)S(1)} collective-permute-done((bf16[8,32,256]{2,1,0:T(8,128)(2,1)S(1)}, bf16[8,32,256]{2,1,0:T(8,128)(2,1)S(1)}, u32[]{:S(2)}, u32[]{:S(2)}) %collective-permute-start.58) | collective-permute-done | bytes 131104 | tf_op jit(solution)/shard_map/spread_slopes/ppermute | solution.py:507
  217.5 9.1 %collective-permute-done.61.refs_3_ = bf16[8,96,256]{2,1,0:T(8,128)(2,1)S(1)} collective-permute-done((bf16[8,96,256]{2,1,0:T(8,128)(2,1)S(1)}, bf16[8,96,256]{2,1,0:T(8,128)(2,1)S(1)}, u32[]{:S(2)}, u32[]{:S(2)}) %collective-permute-start.61) | collective-permute-done | bytes 393248 | tf_op jit(solution)/shard_map/spread_slopes/ppermute | solution.py:33
  226.6 6.4 %collective-permute-done.60.refs_2_ = bf16[8,96,256]{2,1,0:T(8,128)(2,1)} collective-permute-done((bf16[8,96,256]{2,1,0:T(8,128)(2,1)S(1)}, bf16[8,96,256]{2,1,0:T(8,128)(2,1)}, u32[]{:S(2)}, u32[]{:S(2)}) %collective-permute-start.60) | collective-permute-done | bytes 393248 | tf_op jit(solution)/shard_map/spread_slopes/ppermute | solution.py:29
  236.4 4.0 all-to-all-start.1
  246.5 9.6 %weight_taps.3 = (bf16[2,9,64,256]{3,2,1,0:T(8,128)(2,1)}, bf16[2,9,64,256]{3,2,1,0:T(8,128)(2,1)}) custom-call(s32[5]{0:T(128)} %stack.133.info, bf16[8,96,256]{2,1,0:T(8,128)(2,1)} %copy-done.29, bf16[8,96,256]{2,1,0:T(8,128)(2,1)} %collective-permute-done.59.refs_1_, bf16[8,96,256]{2,1,0:T(8,128)(2,1)} %collective-permute-done.60.refs_2_, ...), custom_call_target="tpu_custom_call" | custom-call | flops 8053063680 | bytes 10000000 | tf_op jit(solution)/shard_map/weight_taps/pallas_call | solution.py:456
  257.8 5.6 %collective-permute-done.67.refs_2_.refs_10_ = bf16[8,80,256]{2,1,0:T(8,128)(2,1)} collective-permute-done((bf16[8,80,256]{2,1,0:T(8,128)(2,1)S(1)}, bf16[8,80,256]{2,1,0:T(8,128)(2,1)}, u32[]{:S(2)}, u32[]{:S(2)}) %collective-permute-start.67) | collective-permute-done | bytes 327712 | tf_op jit(solution)/shard_map/spread_slopes/ppermute | solution.py:29
  271.4 10.0 %weight_taps.4 = (bf16[2,9,64,256]{3,2,1,0:T(8,128)(2,1)}, bf16[2,9,64,256]{3,2,1,0:T(8,128)(2,1)}) custom-call(s32[5]{0:T(128)} %stack.133.info, bf16[8,80,256]{2,1,0:T(8,128)(2,1)} %copy-done.30, bf16[8,80,256]{2,1,0:T(8,128)(2,1)} %collective-permute-done.66.refs_1_.refs_9_, bf16[8,80,256]{2,1,0:T(8,128)(2,1)} %collective-permute-done.67.refs_2_.refs_10_, ...), custom_call_target="tpu_custom_call" | custom-call | flops 8053063680 | bytes 10000000 | tf_op jit(solution)/shard_map/weight_taps/pallas_call | solution.py:456
  281.4 3.8 collective-permute-done.74.refs_2_
  290.3 15.0 %input_taps.2.refs_11_ = f32[2,8,128,512]{3,2,1,0:T(8,128)} custom-call(s32[5]{0:T(128)} %stack.133.info, bf16[8,96,256]{2,1,0:T(8,128)(2,1)} %copy-done.29, bf16[8,96,256]{2,1,0:T(8,128)(2,1)} %collective-permute-done.59.refs_1_, bf16[8,96,256]{2,1,0:T(8,128)(2,1)} %collective-permute-done.60.refs_2_, bf16[8,96,256]{2,1,0:T(8,128)(2,1)} %copy-done.78, ...), custom_call_target="tpu_custom_call" | custom-call | flops 10737418240 | bytes 10000000 | tf_op jit(solution)/shard_map/input_grad/input_taps/pallas_call | solution.py:456
  313.3 7.5 %collective-permute-done.89 = bf16[2,9,64,256]{3,2,1,0:T(8,128)(2,1)S(1)} collective-permute-done((bf16[2,9,64,256]{3,2,1,0:T(8,128)(2,1)}, bf16[2,9,64,256]{3,2,1,0:T(8,128)(2,1)S(1)}, u32[]{:S(2)}, u32[]{:S(2)}) %collective-permute-start.89) | collective-permute-done | bytes 589856 | tf_op jit(solution)/shard_map/ppermute | solution.py:820
  327.2 13.1 %weight_taps.5 = (bf16[2,10,64,256]{3,2,1,0:T(8,128)(2,1)}, bf16[2,10,64,256]{3,2,1,0:T(8,128)(2,1)}) custom-call(s32[5]{0:T(128)} %stack.133.info, bf16[8,80,512]{2,1,0:T(8,128)(2,1)} %copy-done.17, bf16[8,80,512]{2,1,0:T(8,128)(2,1)} %collective-permute-done.73.refs_1_, bf16[8,80,512]{2,1,0:T(8,128)(2,1)} %copy-done.39, bf16[8,80,512]{2,1,0:T(8,128)(2,1)} %copy-done.40, ...), custom_call_target="tpu_custom_call" | custom-call | flops 8053063680 | bytes 10000000 | tf_op jit(solution)/shard_map/weight_taps/pallas_call | solution.py:456
  340.6 12.9 %input_taps.3 = (bf16[8,64,512]{2,1,0:T(8,128)(2,1)}, bf16[8,64,512]{2,1,0:T(8,128)(2,1)}, bf16[8,64,512]{2,1,0:T(8,128)(2,1)}, bf16[8,64,512]{2,1,0:T(8,128)(2,1)}) custom-call(s32[5]{0:T(128)} %stack.133.info, bf16[8,80,512]{2,1,0:T(8,128)(2,1)} %copy-done.17, bf16[8,80,512]{2,1,0:T(8,128)(2,1)} %collective-permute-done.73.refs_1_, ...), custom_call_target="tpu_custom_call" | custom-call | flops 10737418240 | bytes 10000000 | tf_op jit(solution)/shard_map/input_grad/input_taps/pallas_call | solution.py:456
  369.2 9.8 %collective-permute-done.92.refs_2_ = bf16[9,64,256]{2,1,0:T(8,128)(2,1)S(1)} collective-permute-done((bf16[9,64,256]{2,1,0:T(8,128)(2,1)S(1)}, bf16[9,64,256]{2,1,0:T(8,128)(2,1)S(1)}, u32[]{:S(2)}, u32[]{:S(2)}) %collective-permute-start.92) | collective-permute-done | bytes 294944 | tf_op jit(solution)/shard_map/ppermute | solution.py:29
  393.9 4.1 collective-permute-done.81.refs_1_
  398.0 11.7 %collective-permute-done.83.refs_3_ = bf16[8,64,512]{2,1,0:T(8,128)(2,1)S(1)} collective-permute-done((bf16[8,64,512]{2,1,0:T(8,128)(2,1)}, bf16[8,64,512]{2,1,0:T(8,128)(2,1)S(1)}, u32[]{:S(2)}, u32[]{:S(2)}) %collective-permute-start.83) | collective-permute-done | bytes 524320 | tf_op jit(solution)/shard_map/input_grad/ppermute | solution.py:33
  413.9 4.1 copy.44
  418.0 3.8 collect.5
  (484 shorter events, 219.8 us)
Async XLA Ops:
  16.8 25.1 %collective-permute-start.4 = (bf16[8,64,512]{2,1,0:T(8,128)(2,1)}, bf16[8,64,512]{2,1,0:T(8,128)(2,1)S(1)}, u32[]{:S(2)}, u32[]{:S(2)}) collective-permute-start(bf16[8,64,512]{2,1,0:T(8,128)(2,1)} %get-tuple-element.123), channel_id=1, source_target_pairs={{0,4},{4,0},{1,5},{5,1},{2,6},{6,2},{3,7},{7,3},{8,12},{12,8},{9,1... | collective-permute-start | bytes 1572872 | tf_op jit(solution)/shard_map/spread_features/ppermute | solution.py:29
  21.2 20.8 %collective-permute-start.5 = (bf16[8,64,512]{2,1,0:T(8,128)(2,1)}, bf16[8,64,512]{2,1,0:T(8,128)(2,1)S(1)}, u32[]{:S(2)}, u32[]{:S(2)}) collective-permute-start(bf16[8,64,512]{2,1,0:T(8,128)(2,1)} %get-tuple-element.124), channel_id=1, source_target_pairs={{0,6},{2,4},{4,2},{6,0},{1,7},{3,5},{5,3},{7,1},{8,14},{10,12},{12... | collective-permute-start | bytes 1572872 | tf_op jit(solution)/shard_map/spread_features/ppermute | solution.py:33
  21.3 21.2 %collective-permute-start.10 = (bf16[4,8,18,512]{3,1,2,0:T(8,128)(2,1)}, bf16[4,8,18,512]{3,1,2,0:T(8,128)(2,1)S(1)}, u32[]{:S(2)}, u32[]{:S(2)}) collective-permute-start(bf16[4,8,18,512]{3,1,2,0:T(8,128)(2,1)} %copy.37), channel_id=1, source_target_pairs={{4,12},{6,14},{8,0},{10,2},{12,20},{14,22},{16,8},{18,10},{20,28},... | collective-permute-start | bytes 1769480 | tf_op jit(solution)/shard_map/spread_features/ppermute | solution.py:507
  38.3 21.4 %collective-permute-start.6 = (bf16[8,64,512]{2,1,0:T(8,128)(2,1)}, bf16[8,64,512]{2,1,0:T(8,128)(2,1)}, u32[]{:S(2)}, u32[]{:S(2)}) collective-permute-start(bf16[8,64,512]{2,1,0:T(8,128)(2,1)} %get-tuple-element.145.refs_0_), channel_id=1, source_target_pairs={{0,1},{1,0},{2,3},{3,2},{4,5},{5,4},{6,7},{7,6},{8,9},{9,8},{10,11... | collective-permute-start | bytes 1572872 | tf_op jit(solution)/shard_map/ppermute | solution.py:29
  72.3 21.6 %collective-permute-start.15 = (bf16[2,8,64,256]{3,2,1,0:T(8,128)(2,1)}, bf16[2,8,64,256]{3,2,1,0:T(8,128)(2,1)S(1)}, u32[]{:S(2)}, u32[]{:S(2)}) collective-permute-start(bf16[2,8,64,256]{3,2,1,0:T(8,128)(2,1)} %get-tuple-element.128), channel_id=1, source_target_pairs={{0,2},{2,0},{1,3},{3,1},{4,6},{6,4},{5,7},{7,5},{8,10},{10,8},{9,1... | collective-permute-start | bytes 1572872 | tf_op jit(solution)/shard_map/ppermute | solution.py:29
  73.8 20.1 %collective-permute-start.16 = (bf16[2,8,64,256]{3,2,1,0:T(8,128)(2,1)}, bf16[2,8,64,256]{3,2,1,0:T(8,128)(2,1)}, u32[]{:S(2)}, u32[]{:S(2)}) collective-permute-start(bf16[2,8,64,256]{3,2,1,0:T(8,128)(2,1)} %get-tuple-element.130), channel_id=1, source_target_pairs={{0,4},{4,0},{1,5},{5,1},{2,6},{6,2},{3,7},{7,3},{8,12},{12,8},{9,1... | collective-permute-start | bytes 1572872 | tf_op jit(solution)/shard_map/ppermute | solution.py:29
  99.4 27.1 %collective-permute-start.19 = (bf16[2,8,64,256]{3,2,1,0:T(8,128)(2,1)}, bf16[2,8,64,256]{3,2,1,0:T(8,128)(2,1)S(1)}, u32[]{:S(2)}, u32[]{:S(2)}) collective-permute-start(bf16[2,8,64,256]{3,2,1,0:T(8,128)(2,1)} %get-tuple-element.142), channel_id=1, source_target_pairs={{0,2},{2,0},{1,3},{3,1},{4,6},{6,4},{5,7},{7,5},{8,10},{10,8},{9,1... | collective-permute-start | bytes 1572872 | tf_op jit(solution)/shard_map/ppermute | solution.py:29
  101.5 25.0 %collective-permute-start.20 = (bf16[2,8,64,256]{3,2,1,0:T(8,128)(2,1)}, bf16[2,8,64,256]{3,2,1,0:T(8,128)(2,1)S(1)}, u32[]{:S(2)}, u32[]{:S(2)}) collective-permute-start(bf16[2,8,64,256]{3,2,1,0:T(8,128)(2,1)} %get-tuple-element.144), channel_id=1, source_target_pairs={{0,4},{4,0},{1,5},{5,1},{2,6},{6,2},{3,7},{7,3},{8,12},{12,8},{9,1... | collective-permute-start | bytes 1572872 | tf_op jit(solution)/shard_map/ppermute | solution.py:29
  213.7 19.3 %collective-permute-start.60 = (bf16[8,96,256]{2,1,0:T(8,128)(2,1)S(1)}, bf16[8,96,256]{2,1,0:T(8,128)(2,1)}, u32[]{:S(2)}, u32[]{:S(2)}) collective-permute-start(bf16[8,96,256]{2,1,0:T(8,128)(2,1)S(1)} %pad_maximum_fusion.2.refs_0_), channel_id=1, source_target_pairs={{0,4},{4,0},{1,5},{5,1},{2,6},{6,2},{3,7},{7,3},{8,12},{12,8},{9,1... | collective-permute-start | bytes 1179656 | tf_op jit(solution)/shard_map/spread_slopes/ppermute | solution.py:29
  217.5 25.4 %collective-permute-start.62 = (bf16[8,96,256]{2,1,0:T(8,128)(2,1)S(1)}, bf16[8,96,256]{2,1,0:T(8,128)(2,1)}, u32[]{:S(2)}, u32[]{:S(2)}) collective-permute-start(bf16[8,96,256]{2,1,0:T(8,128)(2,1)S(1)} %pad_maximum_fusion.2.refs_0_), channel_id=1, source_target_pairs={{0,1},{1,0},{2,3},{3,2},{4,5},{5,4},{6,7},{7,6},{8,9},{9,8},{10,11... | collective-permute-start | bytes 1179656 | tf_op jit(solution)/shard_map/spread_slopes/ppermute | solution.py:29
  236.4 28.4 %all-to-all-start.1 = ((bf16[8,128,256]{2,1,0:T(8,128)(2,1)}), bf16[8,128,256]{2,1,0:T(8,128)(2,1)S(1)}, u32[]{:S(2)}, u32[]{:S(2)}) async-start(bf16[8,128,256]{2,1,0:T(8,128)(2,1)} %bitcast.69), calls=%async_computation.1 | async-start | bytes 1048576 | tf_op jit(solution)/shard_map/spread_slopes/all_to_all | solution.py:772
  243.5 19.9 %collective-permute-start.67 = (bf16[8,80,256]{2,1,0:T(8,128)(2,1)S(1)}, bf16[8,80,256]{2,1,0:T(8,128)(2,1)}, u32[]{:S(2)}, u32[]{:S(2)}) collective-permute-start(bf16[8,80,256]{2,1,0:T(8,128)(2,1)S(1)} %pad_maximum_fusion.4.refs_0_.refs_8_), channel_id=1, source_target_pairs={{0,4},{4,0},{1,5},{5,1},{2,6},{6,2},{3,7},{7,3},{8,12},{12,8},{9,1... | collective-permute-start | bytes 983048 | tf_op jit(solution)/shard_map/spread_slopes/ppermute | solution.py:29
  264.9 42.5 %collective-permute-start.101 = (f32[128,256]{1,0:T(8,128)S(1)}, f32[128,256]{1,0:T(8,128)S(1)}, u32[]{:S(2)}, u32[]{:S(2)}) collective-permute-start(f32[128,256]{1,0:T(8,128)S(1)} %convert_reduce_fusion), channel_id=1, source_target_pairs={{0,24},{8,16},{16,8},{24,0},{1,25},{9,17},{17,9},{25,1},{2,26},{10... | collective-permute-start | bytes 393224 | tf_op jit(solution)/shard_map/project_grad/ppermute | solution.py:38
  267.9 39.6 %collective-permute-start.100 = (f32[128,256]{1,0:T(8,128)S(1)}, f32[128,256]{1,0:T(8,128)}, u32[]{:S(2)}, u32[]{:S(2)}) collective-permute-start(f32[128,256]{1,0:T(8,128)S(1)} %convert_reduce_fusion), channel_id=1, source_target_pairs={{0,16},{8,24},{16,0},{24,8},{1,17},{9,25},{17,1},{25,9},{2,18},{10... | collective-permute-start | bytes 393224 | tf_op jit(solution)/shard_map/project_grad/ppermute | solution.py:38
  268.5 43.2 %collective-permute-start.94 = (bf16[2,9,64,256]{3,2,1,0:T(8,128)(2,1)}, bf16[2,9,64,256]{3,2,1,0:T(8,128)(2,1)S(1)}, u32[]{:S(2)}, u32[]{:S(2)}) collective-permute-start(bf16[2,9,64,256]{3,2,1,0:T(8,128)(2,1)} %get-tuple-element.224), channel_id=1, source_target_pairs={{0,8},{8,0},{16,24},{24,16},{1,9},{9,1},{17,25},{25,17},{2,10},{10... | collective-permute-start | bytes 1769480 | tf_op jit(solution)/shard_map/ppermute | solution.py:820
  307.5 18.0 %collective-permute-start.78 = (bf16[8,80,512]{2,1,0:T(8,128)(2,1)}, bf16[8,80,512]{2,1,0:T(8,128)(2,1)S(1)}, u32[]{:S(2)}, u32[]{:S(2)}) collective-permute-start(bf16[8,80,512]{2,1,0:T(8,128)(2,1)} %collective-permute-done.73.refs_1_), channel_id=1, source_target_pairs={{0,1},{1,0},{2,3},{3,2},{4,5},{5,4},{6,7},{7,6},{8,9},{9,8},{10,11... | collective-permute-start | bytes 1966088 | tf_op jit(solution)/shard_map/ppermute | solution.py:29
  320.8 36.4 %collective-permute-start.95 = (bf16[9,64,256]{2,1,0:T(8,128)(2,1)S(1)}, bf16[9,64,256]{2,1,0:T(8,128)(2,1)}, u32[]{:S(2)}, u32[]{:S(2)}) collective-permute-start(bf16[9,64,256]{2,1,0:T(8,128)(2,1)S(1)} %fusion.39), channel_id=1, source_target_pairs={{0,24},{8,16},{16,8},{24,0},{1,25},{9,17},{17,9},{25,1},{2,26},{10... | collective-permute-start | bytes 884744 | tf_op jit(solution)/shard_map/ppermute | solution.py:823
  324.6 38.9 %collective-permute-start.90 = (bf16[9,64,256]{2,1,0:T(8,128)(2,1)}, bf16[9,64,256]{2,1,0:T(8,128)(2,1)}, u32[]{:S(2)}, u32[]{:S(2)}) collective-permute-start(bf16[9,64,256]{2,1,0:T(8,128)(2,1)} %fusion.38), channel_id=1, source_target_pairs={{0,24},{8,16},{16,8},{24,0},{1,25},{9,17},{17,9},{25,1},{2,26},{10... | collective-permute-start | bytes 884744 | tf_op jit(solution)/shard_map/ppermute | solution.py:823
  360.0 27.0 %all-to-all-start.2 = ((bf16[8,128,256]{2,1,0:T(8,128)(2,1)}), bf16[8,128,256]{2,1,0:T(8,128)(2,1)S(1)}, u32[]{:S(2)}, u32[]{:S(2)}) async-start(bf16[8,128,256]{2,1,0:T(8,128)(2,1)} %broadcast_in_dim.43), calls=%async_computation.2 | async-start | bytes 1048576 | tf_op jit(solution)/shard_map/project_grad/all_to_all | solution.py:923
  367.8 19.0 %collective-permute-start.87 = (bf16[11,64,256]{2,1,0:T(8,128)(2,1)S(1)}, bf16[11,64,256]{2,1,0:T(8,128)(2,1)}, u32[]{:S(2)}, u32[]{:S(2)}) collective-permute-start(bf16[11,64,256]{2,1,0:T(8,128)(2,1)S(1)} %pad_maximum_fusion.3.refs_0_), channel_id=1, source_target_pairs={{0,2},{2,0},{1,3},{3,1},{4,6},{6,4},{5,7},{7,5},{8,10},{10,8},{9,1... | collective-permute-start | bytes 1081352 | tf_op jit(solution)/shard_map/ppermute | solution.py:29
  380.1 17.9 %collective-permute-start.81 = (bf16[8,64,512]{2,1,0:T(8,128)(2,1)}, bf16[8,64,512]{2,1,0:T(8,128)(2,1)S(1)}, u32[]{:S(2)}, u32[]{:S(2)}) collective-permute-start(bf16[8,64,512]{2,1,0:T(8,128)(2,1)} %get-tuple-element.214), channel_id=1, source_target_pairs={{0,2},{2,0},{1,3},{3,1},{4,6},{6,4},{5,7},{7,5},{8,10},{10,8},{9,1... | collective-permute-start | bytes 1572872 | tf_op jit(solution)/shard_map/input_grad/ppermute | solution.py:29
  382.2 27.5 %collective-permute-start.83 = (bf16[8,64,512]{2,1,0:T(8,128)(2,1)}, bf16[8,64,512]{2,1,0:T(8,128)(2,1)S(1)}, u32[]{:S(2)}, u32[]{:S(2)}) collective-permute-start(bf16[8,64,512]{2,1,0:T(8,128)(2,1)} %get-tuple-element.216), channel_id=1, source_target_pairs={{0,6},{2,4},{4,2},{6,0},{1,7},{3,5},{5,3},{7,1},{8,14},{10,12},{12... | collective-permute-start | bytes 1572872 | tf_op jit(solution)/shard_map/input_grad/ppermute | solution.py:33
  383.7 34.3 %collective-permute-start.86 = (bf16[11,64,256]{2,1,0:T(8,128)(2,1)S(1)}, bf16[11,64,256]{2,1,0:T(8,128)(2,1)}, u32[]{:S(2)}, u32[]{:S(2)}) collective-permute-start(bf16[11,64,256]{2,1,0:T(8,128)(2,1)S(1)} %pad_maximum_fusion.3.refs_0_), channel_id=1, source_target_pairs={{0,1},{1,0},{2,3},{3,2},{4,5},{5,4},{6,7},{7,6},{8,9},{9,8},{10,11... | collective-permute-start | bytes 1081352 | tf_op jit(solution)/shard_map/ppermute | solution.py:29
  386.9 31.1 %collective-permute-start.88 = (bf16[11,64,256]{2,1,0:T(8,128)(2,1)}, bf16[11,64,256]{2,1,0:T(8,128)(2,1)}, u32[]{:S(2)}, u32[]{:S(2)}) collective-permute-start(bf16[11,64,256]{2,1,0:T(8,128)(2,1)} %collective-permute-done.87.refs_2_), channel_id=1, source_target_pairs={{0,1},{1,0},{2,3},{3,2},{4,5},{5,4},{6,7},{7,6},{8,9},{9,8},{10,11... | collective-permute-start | bytes 1081352 | tf_op jit(solution)/shard_map/ppermute | solution.py:29
  (161 other events, 2080.2 us)
